TPU v7x, 32 devices: a whole 2x2x4 slice. The times are simulated.
32 devices in a mesh: dp: 2 (over core), mp: 16 (over z, y, x).
Axes of the slice: x: 2, y: 2, z: 4, core: 2. Of those that a mesh axis runs over, the one named last changes fastest.
Arguments:
- rollout_acts: bfloat16 [512, 8192], P(('dp', 'mp')), may hold values from -6 to 6
- gate_pre: bfloat16 [512, 28672], P('dp', 'mp'), may hold values from -6 to 6
- up_pre: bfloat16 [512, 28672], P('dp', 'mp'), may hold values from -6 to 6
- hidden_grad: bfloat16 [512, 28672], P('dp', 'mp'), may hold values from -6 to 6
- row_counts: int32 [2, 16], P('dp'), may hold values from 1 to 16, as said below
- seq_lengths: int32 [2, 4], P('dp'), may hold values from 1 to 112, 224 in all within a row
- tile_owner: int32 [2080], P('mp'), may hold values from 0 to 2079, each once
Outputs:
- act_gram: bfloat16 [2080, 128, 128], P('mp', 'dp')
- grad_gram: bfloat16 [2, 32, 28, 128, 128], P(None, 'mp', None, 'dp')
Inputs may be any that keep to these rules, and one draw needn't show every extreme that they name: In group g the live rows fill the first row_counts[g, j] of the 16 slots of device j; row_counts[g, :] sums to exactly 224, and in each group some device has all 16 slots live. seq_lengths[g, :] sums to exactly 224: the live rows of group g, taken by position, are its 4 sequences in order. `tile_owner`: each tile number appears once.
All inputs are finite; a program needn't handle non-finite values.
Results may differ from a plain program's by a relative error of at most 0.0064.
Values may be sent and summed in bfloat16 or wider, within the bound.
A program may use at most 128 MiB of HBM per device.

v0:
```python
import jax
import jax.numpy as jnp
from jax import lax
from jax.sharding import PartitionSpec as P

TILE = 128
GBLK = 896


def tile_coords(tile_ids, block_count):
    block_ids = jnp.arange(block_count, dtype=jnp.int32)
    starts = block_ids * block_count - block_ids * (block_ids - 1) // 2
    row_block = jnp.sum((tile_ids[:, None] >= starts[None, :]).astype(jnp.int32), axis=1) - 1
    first_tile = jnp.sum(
        jnp.where(block_ids[None, :] == row_block[:, None], starts[None, :], 0), axis=1
    )
    col_block = tile_ids - first_tile + row_block
    return (row_block, col_block)


def slot_weights(counts, lengths, capacity, live_total):
    slot_count = counts.shape[0] * capacity
    slot_ids = jnp.arange(slot_count, dtype=jnp.int32)
    device_ids = jnp.arange(counts.shape[0], dtype=jnp.int32)
    owner_match = (slot_ids // capacity)[:, None] == device_ids[None, :]
    within = slot_ids % capacity
    count_here = jnp.sum(jnp.where(owner_match, counts[None, :], 0), axis=1)
    before = jnp.cumsum(counts) - counts
    offset = jnp.sum(jnp.where(owner_match, before[None, :], 0), axis=1)
    live_mask = within < count_here
    position = offset + within
    seq_ends = jnp.cumsum(lengths)
    seq_match = (position[:, None] < seq_ends[None, :]) & (
        position[:, None] >= (seq_ends - lengths)[None, :]
    )
    own_length = jnp.sum(jnp.where(seq_match, lengths[None, :], 0), axis=1)
    own_length = jnp.maximum(own_length, 1)
    ratio = live_total / lengths.shape[0]
    weight = jnp.where(live_mask, ratio / own_length.astype(jnp.float32), 0.0)
    return (live_mask, position, weight)


def owned_tiles(columns_rows, row_block, col_block):
    row_count = columns_rows.shape[1]
    shaped = columns_rows.reshape(columns_rows.shape[0] // TILE, TILE, row_count)
    left_rows = jnp.take(shaped, row_block, axis=0)
    right_rows = jnp.take(shaped, col_block, axis=0)
    return jnp.einsum("kin,kjn->kij", left_rows, right_rows, preferred_element_type=jnp.float32)


def gradient_tiles(gate_rows, up_rows, cot_rows, row_weight, row_scale):
    gate_value = gate_rows.astype(jnp.float32)
    up_value = up_rows.astype(jnp.float32)
    hidden_cot = cot_rows.astype(jnp.float32)
    sigmoid_gate = jax.nn.sigmoid(gate_value)
    gate_grad = hidden_cot * up_value * sigmoid_gate * (1.0 + gate_value * (1.0 - sigmoid_gate))
    up_grad = hidden_cot * gate_value * sigmoid_gate
    weight_col = row_weight[:, None]
    scaled_pair = (
        (gate_grad * weight_col).astype(jnp.bfloat16),
        (up_grad * weight_col).astype(jnp.bfloat16),
    )
    per_device = gate_rows.shape[1] // GBLK
    span = GBLK // TILE
    pieces = []
    for which in range(2):
        scaled = scaled_pair[which]
        for block in range(per_device):
            for strip in range(span):
                first = block * GBLK + strip * TILE
                left_cols = scaled[:, first : first + TILE]
                right_cols = scaled[:, first : (block + 1) * GBLK]
                product = (
                    lax.dot_general(
                        left_cols,
                        right_cols,
                        (((0,), (0,)), ((), ())),
                        preferred_element_type=jnp.float32,
                    )
                    * row_scale
                )
                pieces.append(product.reshape(TILE, span - strip, TILE).transpose(1, 0, 2))
    return jnp.concatenate(pieces, axis=0)


def body(rollout_acts, gate_pre, up_pre, hidden_grad, row_counts, seq_lengths, tile_owner):
    mp_size = lax.axis_size("mp")
    dp_size = lax.axis_size("dp")
    capacity = rollout_acts.shape[0]
    slot_count = mp_size * capacity
    live_total = slot_count - 2 * capacity
    row_scale = 1.0 / (dp_size * live_total)
    live_mask, position, weight = slot_weights(row_counts[0], seq_lengths[0], capacity, live_total)
    row_block, col_block = tile_coords(tile_owner, rollout_acts.shape[1] // TILE)
    grad_tiles = gradient_tiles(gate_pre, up_pre, hidden_grad, weight, row_scale)
    own_columns = rollout_acts.T
    gathered = lax.all_gather(own_columns, "mp", axis=1, tiled=True)
    used_cols = gathered * live_mask[None, :].astype(jnp.bfloat16)
    act_tiles = owned_tiles(used_cols, row_block, col_block) * row_scale
    act_sum, grad_sum = (
        lax.psum_scatter(
            act_tiles.astype(jnp.bfloat16), "dp", scatter_dimension=1, tiled=True
        ).astype(jnp.float32),
        lax.psum_scatter(
            grad_tiles.astype(jnp.bfloat16), "dp", scatter_dimension=1, tiled=True
        ).astype(jnp.float32),
    )
    act_gram = act_sum.astype(jnp.bfloat16)
    per_device = gate_pre.shape[1] // GBLK
    tile_pairs = grad_sum.shape[0] // (2 * per_device)
    grad_gram = grad_sum.astype(jnp.bfloat16).reshape(
        2, per_device, tile_pairs, grad_sum.shape[1], TILE
    )
    return (act_gram, grad_gram)


def solution(mesh):
    return jax.shard_map(
        body,
        mesh=mesh,
        in_specs=(
            P(("dp", "mp"), None),
            P("dp", "mp"),
            P("dp", "mp"),
            P("dp", "mp"),
            P("dp", None),
            P("dp", None),
            P("mp"),
        ),
        out_specs=(P("mp", "dp", None), P(None, "mp", None, "dp", None)),
        check_vma=False,
    )
```

profile of v0, /device:TPU:0, one launch (start us, length us, event | category | flops | bytes accessed | tf_op | source)
XLA Modules:
  0.0 146.6 jit_solution(12933135869681737857)
XLA Ops:
  8.0 0.7 all-gather.2.cloned.1.call-update
  8.8 0.8 reduce-window_clone.1
  9.6 0.7 subtract_bitcast_fusion
  10.3 0.7 select_reduce_fusion.1
  11.0 0.8 reduce-window.6
  11.9 0.7 fusion.107
  12.5 0.7 select_reduce_fusion.3
  13.3 2.8 %fusion.20 = (bf16[256,1792]{1,0:T(8,128)(2,1)S(1)}, bf16[256,1792]{1,0:T(8,128)(2,1)S(1)}) fusion(bf16[256,1792]{1,0:T(8,128)(2,1)} %param.10, bf16[256,1792]{1,0:T(8,128)(2,1)} %param.12, f32[256]{0:T(256)S(1)} %divide_select_fusion, bf16[256,1792]{1,0:T(8,128)(2,1)} %param.11), kind=kLoop, calls=%fused_computation.24 | loop fusion | flops 8257536 | bytes 4588544 | tf_op jit(solution)/shard_map/convert_element_type | solution.py:61
  18.2 0.8 copy.137
  18.9 0.7 copy.111
  19.7 0.7 copy.138
  20.4 0.7 copy.131
  22.6 0.8 copy.139
  23.6 0.8 copy.117
  24.5 0.7 copy.140
  27.0 0.7 copy.141
  28.0 0.7 copy.123
  28.9 0.7 copy.142
  29.9 0.7 copy.133
  31.4 0.9 fusion.32
  32.3 1.1 copy.127
  33.6 0.8 copy.143
  34.6 0.8 copy.129
  35.4 0.8 fusion.44
  36.2 1.6 %copy.144 = bf16[128,256]{0,1:T(8,128)(2,1)} copy(bf16[128,256]{1,0:T(8,128)(2,1)} %fusion.44) | data formatting | bytes 131072 | tf_op jit(solution)/shard_map/reshape | solution.py:82
  37.8 0.8 fusion.49
  38.6 0.9 copy.134
  39.5 0.7 constant_dynamic-update-slice_fusion.27
  40.2 0.7 constant_dynamic-update-slice_fusion.26
  40.8 0.7 constant_dynamic-update-slice_fusion.25
  41.5 1.6 %constant_dynamic-update-slice_fusion.24 = bf16[112,128,128]{1,2,0:T(8,128)(2,1)} fusion(bf16[112,128,128]{1,2,0:T(8,128)(2,1)} %constant_dynamic-update-slice_fusion.25, bf16[4,128,128]{1,2,0:T(8,128)(2,1)} %bitcast.113), kind=kLoop, calls=%fused_computation.164 | loop fusion | bytes 262144
  43.1 1.5 %constant_dynamic-update-slice_fusion.23 = bf16[112,128,128]{1,2,0:T(8,128)(2,1)} fusion(bf16[112,128,128]{1,2,0:T(8,128)(2,1)} %constant_dynamic-update-slice_fusion.24, bf16[3,128,128]{1,2,0:T(8,128)(2,1)} %bitcast.115), kind=kLoop, calls=%fused_computation.163 | loop fusion | bytes 196608
  44.6 1.5 constant_dynamic-update-slice_fusion.22
  46.1 0.6 constant_dynamic-update-slice_fusion.21
  46.7 0.7 constant_dynamic-update-slice_fusion.20
  47.4 0.7 constant_dynamic-update-slice_fusion.19
  48.1 0.7 constant_dynamic-update-slice_fusion.18
  48.8 1.6 %constant_dynamic-update-slice_fusion.17 = bf16[112,128,128]{1,2,0:T(8,128)(2,1)} fusion(bf16[112,128,128]{1,2,0:T(8,128)(2,1)} %constant_dynamic-update-slice_fusion.18, bf16[4,128,128]{1,2,0:T(8,128)(2,1)} %bitcast.110), kind=kLoop, calls=%fused_computation.157 | loop fusion | bytes 262144
  50.3 1.5 %constant_dynamic-update-slice_fusion.16 = bf16[112,128,128]{1,2,0:T(8,128)(2,1)} fusion(bf16[112,128,128]{1,2,0:T(8,128)(2,1)} %constant_dynamic-update-slice_fusion.17, bf16[3,128,128]{1,2,0:T(8,128)(2,1)} %bitcast.114), kind=kLoop, calls=%fused_computation.156 | loop fusion | bytes 196608
  51.9 1.5 %constant_dynamic-update-slice_fusion.15 = bf16[112,128,128]{1,2,0:T(8,128)(2,1)} fusion(bf16[112,128,128]{1,2,0:T(8,128)(2,1)} %constant_dynamic-update-slice_fusion.16, bf16[2,128,128]{1,2,0:T(8,128)(2,1)} %bitcast.119), kind=kLoop, calls=%fused_computation.155 | loop fusion | bytes 131072
  53.3 0.6 constant_dynamic-update-slice_fusion.14
  53.9 0.7 constant_dynamic-update-slice_fusion.13
  54.7 0.7 constant_dynamic-update-slice_fusion.12
  55.4 0.7 constant_dynamic-update-slice_fusion.11
  56.0 1.6 %constant_dynamic-update-slice_fusion.10 = bf16[112,128,128]{1,2,0:T(8,128)(2,1)} fusion(bf16[112,128,128]{1,2,0:T(8,128)(2,1)} %constant_dynamic-update-slice_fusion.11, bf16[4,128,128]{1,2,0:T(8,128)(2,1)} %bitcast.111), kind=kLoop, calls=%fused_computation.150 | loop fusion | bytes 262144
  57.6 1.5 %constant_dynamic-update-slice_fusion.9 = bf16[112,128,128]{1,2,0:T(8,128)(2,1)} fusion(bf16[112,128,128]{1,2,0:T(8,128)(2,1)} %constant_dynamic-update-slice_fusion.10, bf16[3,128,128]{1,2,0:T(8,128)(2,1)} %bitcast.116), kind=kLoop, calls=%fused_computation.149 | loop fusion | bytes 196608
  59.1 1.5 %constant_dynamic-update-slice_fusion.8 = bf16[112,128,128]{1,2,0:T(8,128)(2,1)} fusion(bf16[112,128,128]{1,2,0:T(8,128)(2,1)} %constant_dynamic-update-slice_fusion.9, bf16[2,128,128]{1,2,0:T(8,128)(2,1)} %bitcast.121), kind=kLoop, calls=%fused_computation.148 | loop fusion | bytes 131072
  60.6 0.6 constant_dynamic-update-slice_fusion.7
  61.2 0.7 constant_dynamic-update-slice_fusion.6
  61.9 0.7 constant_dynamic-update-slice_fusion.5
  62.6 0.7 constant_dynamic-update-slice_fusion.4
  63.3 0.7 constant_dynamic-update-slice_fusion.3
  64.0 1.5 %constant_dynamic-update-slice_fusion.2 = bf16[112,128,128]{1,2,0:T(8,128)(2,1)} fusion(bf16[112,128,128]{1,2,0:T(8,128)(2,1)} %constant_dynamic-update-slice_fusion.3, bf16[3,128,128]{1,2,0:T(8,128)(2,1)} %bitcast.117), kind=kLoop, calls=%fused_computation.142 | loop fusion | bytes 196608
  65.5 0.6 constant_dynamic-update-slice_fusion.1
  66.1 0.6 constant_dynamic-update-slice_fusion
  66.7 6.1 %copy.135 = bf16[112,128,128]{2,0,1:T(8,128)(2,1)} copy(bf16[112,128,128]{1,2,0:T(8,128)(2,1)} %constant_dynamic-update-slice_fusion) | data formatting | bytes 7340032 | tf_op jit(solution)/shard_map/concatenate | solution.py:83
  73.8 16.8 %all-gather.2.cloned.1.call-done = bf16[8192,256]{0,1:T(8,128)(2,1)} async-done(((bf16[8192,16]{0,1:T(8,128)(2,1)}), bf16[8192,256]{0,1:T(8,128)(2,1)}) %all-gather.2.cloned.1.call-update) | async-done | bytes 4194320 | tf_op jit(solution)/shard_map/all_gather | solution.py:97
  90.6 4.5 %broadcast_multiply_fusion = bf16[8192,256]{0,1:T(8,128)(2,1)} fusion(bf16[8192,256]{0,1:T(8,128)(2,1)} %all-gather.2.cloned.1.call-done, bf16[256]{0:T(256)(128)(2,1)S(1)} %fusion.111), kind=kLoop, calls=%fused_computation.13 | loop fusion | flops 2097152 | bytes 8389120 | tf_op jit(solution)/shard_map/mul | solution.py:98
  95.1 6.4 %copy.106 = bf16[8192,256]{1,0:T(8,128)(2,1)} copy(bf16[8192,256]{0,1:T(8,128)(2,1)} %broadcast_multiply_fusion) | data formatting | bytes 8388608 | tf_op jit(solution)/shard_map/mul | solution.py:98
  101.5 9.2 %gather_fusion.1 = bf16[130,128,256]{2,1,0:T(8,128)(2,1)} fusion(bf16[64,128,256]{2,1,0:T(8,128)(2,1)} %bitcast.95, s32[1024]{0:T(1024)S(1)} %get-tuple-element.16), kind=kCustom, calls=%fused_computation.1.clone | custom fusion | bytes 17039880 | tf_op jit(solution)/shard_map/jit(_take)/gather | solution.py:47
  110.6 9.1 %gather_fusion = bf16[130,128,256]{2,1,0:T(8,128)(2,1)} fusion(bf16[64,128,256]{2,1,0:T(8,128)(2,1)} %bitcast.96, s32[1024]{0:T(1024)S(1)} %get-tuple-element.17), kind=kCustom, calls=%fused_computation.clone | custom fusion | bytes 17039880 | tf_op jit(solution)/shard_map/jit(_take)/gather | solution.py:46
  119.7 8.7 %multiply_convert_fusion = bf16[130,128,128]{2,1,0:T(8,128)(2,1)} fusion(bf16[130,128,256]{2,1,0:T(8,128)(2,1)} %gather_fusion.1, pred[130]{0:T(512)(128)(4,1)S(1)} %get-tuple-element.9, bf16[130,128,256]{2,1,0:T(8,128)(2,1)} %gather_fusion, pred[130]{0:T(512)(128)(4,1)S(1)} %get-tuple-element.13), kind=kOutput, calls=%fused_computation.5 | convolution fusion | flops 1103298560 | bytes 21299460 | tf_op jit(solution)/shard_map/kin,kjn->kij/dot_general | solution.py:48
  128.5 3.2 %copy.136 = bf16[112,64,128]{2,1,0:T(8,128)(2,1)} copy(bf16[112,64,128]{2,0,1:T(8,128)(2,1)} %reduce-scatter.5.cloned.1.call-done) | data formatting | bytes 3670016 | tf_op jit(solution)/shard_map/reduce_scatter | solution.py:104
  131.7 7.5 %reduce-scatter.3.cloned.1.call-done = bf16[130,64,128]{2,1,0:T(8,128)(2,1)} async-done(((bf16[130,128,128]{2,1,0:T(8,128)(2,1)}), bf16[130,64,128]{2,1,0:T(8,128)(2,1)}) %reduce-scatter.3.cloned.1.call-update) | async-done | bytes 2129936 | tf_op jit(solution)/shard_map/reduce_scatter | solution.py:101
  (63 shorter events, 8.5 us)
Async XLA Ops:
  8.0 82.6 %all-gather.2.cloned.1.call-start = ((), (), s32[]{:S(2)}) async-start(), calls=%async_computation.2 | async-start | bytes 4456448 | tf_op jit(solution)/shard_map/all_gather | solution.py:97
  8.7 119.7 %reduce-scatter.5.cloned.1.call-start = ((), (), s32[]{:S(2)}) async-start(), calls=%async_computation.4 | async-start | bytes 5505024 | tf_op jit(solution)/shard_map/reduce_scatter | solution.py:104
  28.7 17.3 %copy-start.2 = (bf16[1,128,128]{1,2,0:T(8,128)(2,1)S(1)}, bf16[1,128,128]{1,2,0:T(8,128)(2,1)}, u32[]{:S(2)}) copy-start(bf16[1,128,128]{1,2,0:T(8,128)(2,1)} %copy.131) | copy-start | bytes 98308
  33.4 27.2 %copy-start.3 = (bf16[1,128,128]{1,2,0:T(8,128)(2,1)S(1)}, bf16[1,128,128]{1,2,0:T(8,128)(2,1)}, u32[]{:S(2)}) copy-start(bf16[1,128,128]{1,2,0:T(8,128)(2,1)} %copy.133) | copy-start | bytes 98308
  35.4 28.0 %copy-start = (bf16[128,512]{0,1:T(8,128)(2,1)S(1)}, bf16[128,512]{0,1:T(8,128)(2,1)}, u32[]{:S(2)}) copy-start(bf16[128,512]{0,1:T(8,128)(2,1)} %copy.143) | copy-start | bytes 393220
  38.6 26.9 %copy-start.1 = (bf16[128,256]{0,1:T(8,128)(2,1)S(1)}, bf16[128,256]{0,1:T(8,128)(2,1)}, u32[]{:S(2)}) copy-start(bf16[128,256]{0,1:T(8,128)(2,1)} %copy.144) | copy-start | bytes 196612
  72.9 0.7 copy-start.4
  72.9 66.3 %reduce-scatter.3.cloned.1.call-start = ((), (), s32[]{:S(2)}) async-start(), calls=%async_computation.3 | async-start | bytes 6389760 | tf_op jit(solution)/shard_map/reduce_scatter | solution.py:101
Sparse Core Ops, SparseCore 0:
  12.0 78.5 all-gather.1
Sparse Core Ops, SparseCore 1:
  73.0 14.2 reduce-scatter.4
  128.5 10.6 reduce-scatter.2
where the time goes:
time: 148 us; the launch traced here: 147 us
  local copies, waits for them, and re-layouts  76.8 us (52%)
  waiting for transfers between devices  25.1 us (17%)
  matrix products  16.7 us (11%)
  between operations  15.7 us (11%)
  other arithmetic  12 us (8%)
    unnamed x37, local copies, waits for them, and re-layouts  27.1 us
    all_gather x1, waiting for transfers between devices, body(): gathered = lax.all_gather(own_columns, 'mp', axis=1, tiled=True)  16.8 us
    gather x1, local copies, waits for them, and re-layouts, owned_tiles(): right_rows = jnp.take(shaped, col_block, axis=0)  9.17 us
    gather x1, local copies, waits for them, and re-layouts, owned_tiles(): left_rows = jnp.take(shaped, row_block, axis=0)  9.1 us
    dot_general x1, matrix products, owned_tiles(): jnp.einsum('kin,kjn->kij', left_rows, right_rows, preferred_element_type=...  8.68 us
    dot_general x28, matrix products, gradient_tiles(): lax.dot_general(left_cols, right_cols, (((0,), (0,)), ((), ())), preferre...  8.06 us
    reduce_scatter x1, waiting for transfers between devices, body(): lax.psum_scatter(act_tiles.astype(jnp.bfloat16), 'dp', scatter_dimension=...  7.52 us
    reshape x8, local copies, waits for them, and re-layouts, gradient_tiles(): pieces.append(product.reshape(TILE, span - strip, TILE).transpose(1, 0, 2))  6.74 us
  transfers between devices with their start and end apart: 3, of which 2 were waited for; matrix products, arithmetic and copies ran while one was open for 72% of the time, Pallas kernels for 0%

commit v1 on v0

v1 whole, which is shorter than its diff:
```python
import functools

import jax
import jax.numpy as jnp
from jax import lax
from jax.experimental import pallas as pl
from jax.experimental.pallas import tpu as pltpu
from jax.sharding import PartitionSpec as P

TILE = 128
GBLK = 896
MESH = pl.DeviceIdType.MESH
F32 = jnp.float32
BF16 = jnp.bfloat16


def largest_divisor(number, limit):
    return max(d for d in range(1, limit + 1) if number % d == 0)


def fused_kernel(
    scale,
    ratio,
    act_in,
    gate_in,
    up_in,
    hid_in,
    counts,
    lengths,
    owner,
    act_out,
    grad_out,
    own_raw,
    gate,
    up,
    hid,
    xs,
    xt,
    sc,
    sct,
    wt,
    rb,
    cb,
    part_a,
    recv_a,
    part_g,
    recv_g,
    stage_a,
    stage_g,
    in_sem,
    out_a_sem,
    out_g_sem,
    zs,
    zr,
    fs,
    fr,
    hs,
    hr,
    gs,
    gr,
    as_,
    ar,
):
    g = lax.axis_index("dp")
    me = lax.axis_index("mp")
    z = me // 4
    y = (me // 2) % 2
    x = me % 2
    xy = me % 4
    xn = me + 1 - 2 * x
    yn = me + 2 - 4 * y
    z1 = z + 1 - 2 * (z % 2)
    z2 = (z + 2) % 4
    z3 = 3 - z
    mid = ((z + 1) // 2) % 2
    is_mid = mid == 1
    zorder = (z, z1, mid * z3 + (1 - mid) * z2, mid * z2 + (1 - mid) * z3)
    cap = act_in.shape[0]
    blocks = xs.shape[1]
    half = blocks // 2
    xy_of_xn = y * 2 + (1 - x)
    xy_of_yn = (1 - y) * 2 + x
    xy_of_d = (1 - y) * 2 + (1 - x)

    loads = [
        pltpu.make_async_copy(act_in, own_raw, in_sem.at[0]),
        pltpu.make_async_copy(gate_in, gate, in_sem.at[1]),
        pltpu.make_async_copy(up_in, up, in_sem.at[2]),
        pltpu.make_async_copy(hid_in, hid, in_sem.at[3]),
    ]
    for copy in loads:
        copy.start()

    loads[0].wait()
    live = counts[0, me]
    row_live = lax.broadcasted_iota(jnp.int32, (cap, TILE), 0) < live

    def put_own(b, carry):
        value = own_raw[:, pl.ds(pl.multiple_of(b * TILE, TILE), TILE)]
        xs[me, b] = jnp.where(row_live, value.astype(F32), 0.0).astype(BF16)
        return carry

    lax.fori_loop(0, blocks, put_own, 0, unroll=8)

    barrier = pltpu.get_barrier_semaphore()
    for other in ((1 - g, me), (g, xn), (g, yn), (g, z1 * 4 + xy)):
        pl.semaphore_signal(barrier, inc=1, device_id=other, device_id_type=MESH)

    @pl.when(is_mid)
    def _():
        pl.semaphore_signal(
            barrier, inc=1, device_id=(g, z3 * 4 + xy), device_id_type=MESH
        )

    pl.semaphore_wait(barrier, 4 + mid)

    def z_copy(src_z, target_z, index, which):
        slot = xs.at[src_z * 4 + xy]
        return pltpu.make_async_remote_copy(
            src_ref=slot, dst_ref=slot, send_sem=zs.at[index], recv_sem=zr.at[which],
            device_id=(g, target_z * 4 + xy), device_id_type=MESH,
        )

    def full_copy(way, item, slot_xy, target):
        slot = xs.at[zorder[item] * 4 + slot_xy]
        return pltpu.make_async_remote_copy(
            src_ref=slot, dst_ref=slot, send_sem=fs.at[way, item], recv_sem=fr.at[way, item],
            device_id=(g, target), device_id_type=MESH,
        )

    def half_copy(way, item, slot_xy, target):
        slot = xs.at[zorder[item] * 4 + slot_xy, pl.ds(way * half, half)]
        return pltpu.make_async_remote_copy(
            src_ref=slot, dst_ref=slot, send_sem=hs.at[way, item], recv_sem=hr.at[way, item],
            device_id=(g, target), device_id_type=MESH,
        )

    def send_item(item):
        full_copy(0, item, xy, xn).start()
        full_copy(1, item, xy, yn).start()

    def pass_halves(item):
        full_copy(1, item, xy_of_yn, yn).wait_recv()
        half_copy(0, item, xy_of_yn, xn).start()
        full_copy(0, item, xy_of_xn, xn).wait_recv()
        half_copy(1, item, xy_of_xn, yn).start()

    def take_halves(item):
        half_copy(0, item, xy_of_d, xn).wait_recv()
        half_copy(1, item, xy_of_d, yn).wait_recv()

    z_copy(z, z1, 0, 0).start()
    send_item(0)

    @pl.when(is_mid)
    def _():
        z_copy(z, z3, 1, 1).start()

    within = lax.broadcasted_iota(jnp.int32, (cap, TILE), 0)
    seqs = lengths.shape[1]

    def put_weight(j, offset):
        here = counts[0, j]
        position = within + offset
        own = jnp.ones((cap, TILE), jnp.int32)
        start = jnp.int32(0)
        for k in range(seqs):
            size = lengths[0, k]
            inside = (position >= start) & (position < start + size)
            own = jnp.where(inside, size, own)
            start = start + size
        own = jnp.maximum(own, 1).astype(F32)
        wt[pl.ds(pl.multiple_of(j * cap, cap), cap), :] = jnp.where(
            within < here, ratio / own, 0.0
        )
        return offset + here

    lax.fori_loop(0, counts.shape[1], put_weight, jnp.int32(0))

    for copy in loads[1:]:
        copy.wait()
    per = sc.shape[1]
    span = GBLK // TILE
    rows = gate.shape[0]
    chunk = 64

    def scaled_block(n, carry):
        m = n // span
        for c in range(rows // chunk):
            rs = slice(c * chunk, (c + 1) * chunk)
            cols = pl.ds(pl.multiple_of(n * TILE, TILE), TILE)
            a = gate[rs, cols].astype(F32)
            b = up[rs, cols].astype(F32)
            h = hid[rs, cols].astype(F32)
            w = wt[rs, :]
            q = 0.5 * jnp.tanh(0.5 * a) + 0.5
            hq = h * q
            gate_grad = hq * b * (1.0 + a * (1.0 - q))
            up_grad = hq * a
            sc[0, m, n % span, rs, :] = (gate_grad * w).astype(BF16)
            sc[1, m, n % span, rs, :] = (up_grad * w).astype(BF16)
        for e in range(2):
            sct[e, m, n % span] = sc[e, m, n % span].T
        return carry

    lax.fori_loop(0, per * span, scaled_block, 0)

    z_copy(z1, z1, 0, 0).wait_recv()
    send_item(1)

    @pl.when(is_mid)
    def _():
        z_copy(z1, z3, 2, 2).start()

    pass_halves(0)

    pairs = [(i, j) for i in range(span) for j in range(i, span)]
    other_rows = pl.ds(pl.multiple_of(64 * (1 - g), 64), 64)
    own_rows = pl.ds(pl.multiple_of(64 * g, 64), 64)

    def grad_send(q):
        return pltpu.make_async_remote_copy(
            src_ref=part_g.at[q, :, other_rows], dst_ref=recv_g.at[q],
            send_sem=gs.at[q], recv_sem=gr.at[q],
            device_id=(1 - g, me), device_id_type=MESH,
        )

    def grad_tiles(q, carry):
        e = q // per
        m = q % per
        for k, (i, j) in enumerate(pairs):
            tile = jnp.dot(sct[e, m, i], sc[e, m, j], preferred_element_type=F32)
            part_g[q, k] = (tile * scale).astype(BF16)
        grad_send(q).start()
        return carry

    lax.fori_loop(0, 2 * per, grad_tiles, 0)

    z_copy(zorder[2], z1, 0, 1).wait_recv()
    send_item(2)

    @pl.when(is_mid)
    def _():
        z_copy(z3, z1, 1 + 2, 1).start()

    pass_halves(1)

    z_copy(zorder[3], z1, 0, 2).wait_recv()
    send_item(3)

    @pl.when(is_mid)
    def _():
        z_copy(z2, z1, 4, 2).start()

    tiles = owner.shape[0]

    def put_coords(k, carry):
        t = owner[k]
        r = jnp.int32(0)
        step = 1
        while step * 2 < blocks:
            step *= 2
        while step:
            cand = r + step
            begin = cand * blocks - (cand * (cand - 1)) // 2
            r = jnp.where((cand < blocks) & (t >= begin), cand, r)
            step //= 2
        rb[k] = r
        cb[k] = t - (r * blocks - (r * (r - 1)) // 2) + r
        return carry

    lax.fori_loop(0, tiles, put_coords, 0)

    def grad_out_copy(q):
        return pltpu.make_async_copy(
            stage_g.at[q], grad_out.at[q // per, q % per], out_g_sem.at[q]
        )

    def grad_finish(q, carry):
        grad_send(q).wait()
        for k in range(len(pairs)):
            total = part_g[q, k, own_rows].astype(F32) + recv_g[q, k].astype(F32)
            stage_g[q, k] = total.astype(BF16)
        grad_out_copy(q).start()
        return carry

    take_halves(0)
    take_halves(1)

    group = 8

    def transpose_half(which):
        def one(b, carry):
            block = xs[pl.ds(which * group, group), b].reshape(group * cap, TILE)
            xt[b, :, pl.ds(pl.multiple_of(which * TILE, TILE), TILE)] = block.T
            return carry

        lax.fori_loop(0, blocks, one, 0, unroll=4)

    pass_halves(2)
    lax.fori_loop(0, 2 * per, grad_finish, 0)
    pass_halves(3)
    take_halves(2)
    take_halves(3)
    transpose_half(0)
    transpose_half(1)

    chunks = part_a.shape[0]
    width = part_a.shape[1]

    def act_send(n):
        return pltpu.make_async_remote_copy(
            src_ref=part_a.at[n, :, other_rows], dst_ref=recv_a.at[n],
            send_sem=as_.at[n], recv_sem=ar.at[n],
            device_id=(1 - g, me), device_id_type=MESH,
        )

    def act_out_copy(n):
        return pltpu.make_async_copy(
            stage_a.at[n], act_out.at[pl.ds(n * width, width)], out_a_sem.at[n]
        )

    def act_tiles(n, carry):
        for i in range(width):
            k = n * width + i
            left = xt[rb[k]]
            right = xs[:, cb[k]].reshape(2 * TILE, TILE)
            tile = jnp.dot(left, right, preferred_element_type=F32)
            part_a[n, i] = (tile * scale).astype(BF16)
        act_send(n).start()
        return carry

    def act_finish(n, carry):
        act_send(n).wait()
        for i in range(width):
            total = part_a[n, i, own_rows].astype(F32) + recv_a[n, i].astype(F32)
            stage_a[n, i] = total.astype(BF16)
        act_out_copy(n).start()
        return carry

    def act_both(n, carry):
        act_tiles(n, carry)
        act_finish(n - 2, carry)
        return carry

    lax.fori_loop(0, 2, act_tiles, 0)
    lax.fori_loop(2, chunks, act_both, 0)
    lax.fori_loop(chunks - 2, chunks, act_finish, 0)

    z_copy(z, z1, 0, 0).wait_send()

    @pl.when(is_mid)
    def _():
        z_copy(z, z3, 1, 1).wait_send()
        z_copy(z1, z3, 2, 2).wait_send()
        z_copy(z3, z1, 3, 1).wait_send()
        z_copy(z2, z1, 4, 2).wait_send()

    for item in range(4):
        full_copy(0, item, xy, xn).wait_send()
        full_copy(1, item, xy, yn).wait_send()
        half_copy(0, item, xy_of_yn, xn).wait_send()
        half_copy(1, item, xy_of_xn, yn).wait_send()

    def wait_grad_out(q, carry):
        grad_out_copy(q).wait()
        return carry

    def wait_act_out(n, carry):
        act_out_copy(n).wait()
        return carry

    lax.fori_loop(0, 2 * per, wait_grad_out, 0)
    lax.fori_loop(0, chunks, wait_act_out, 0)


def fused_body(acts, gate, up, hid, counts, lengths, owner):
    cap, width = acts.shape
    slots = 16
    rows = slots * cap
    live_total = rows - 2 * cap
    blocks = width // TILE
    tiles = owner.shape[0]
    per = gate.shape[1] // GBLK
    span = GBLK // TILE
    pairs = span * (span + 1) // 2
    chunk = largest_divisor(tiles, 10)
    chunks = tiles // chunk
    anywhere = pl.BlockSpec(memory_space=pl.ANY)
    smem = pl.BlockSpec(memory_space=pltpu.SMEM)
    dma = pltpu.SemaphoreType.DMA
    kernel = functools.partial(
        fused_kernel, 1.0 / (2 * live_total), live_total / lengths.shape[1]
    )
    return pl.pallas_call(
        kernel,
        out_shape=(
            jax.ShapeDtypeStruct((tiles, TILE // 2, TILE), BF16),
            jax.ShapeDtypeStruct((2, per, pairs, TILE // 2, TILE), BF16),
        ),
        in_specs=[anywhere] * 4 + [smem] * 3,
        out_specs=(anywhere, anywhere),
        scratch_shapes=[
            pltpu.VMEM((cap, width), BF16),
            pltpu.VMEM(gate.shape, BF16),
            pltpu.VMEM(gate.shape, BF16),
            pltpu.VMEM(gate.shape, BF16),
            pltpu.VMEM((slots, blocks, cap, TILE), BF16),
            pltpu.VMEM((blocks, TILE, rows), BF16),
            pltpu.VMEM((2, per, span, rows, TILE), BF16),
            pltpu.VMEM((2, per, span, TILE, rows), BF16),
            pltpu.VMEM((rows, TILE), F32),
            pltpu.SMEM((tiles,), jnp.int32),
            pltpu.SMEM((tiles,), jnp.int32),
            pltpu.VMEM((chunks, chunk, TILE, TILE), BF16),
            pltpu.VMEM((chunks, chunk, TILE // 2, TILE), BF16),
            pltpu.VMEM((2 * per, pairs, TILE, TILE), BF16),
            pltpu.VMEM((2 * per, pairs, TILE // 2, TILE), BF16),
            pltpu.VMEM((chunks, chunk, TILE // 2, TILE), BF16),
            pltpu.VMEM((2 * per, pairs, TILE // 2, TILE), BF16),
            dma((4,)),
            dma((chunks,)),
            dma((2 * per,)),
            dma((5,)),
            dma((3,)),
            dma((2, 4)),
            dma((2, 4)),
            dma((2, 4)),
            dma((2, 4)),
            dma((2 * per,)),
            dma((2 * per,)),
            dma((chunks,)),
            dma((chunks,)),
        ],
        compiler_params=pltpu.CompilerParams(
            collective_id=0, has_side_effects=True, vmem_limit_bytes=50 * 2**20
        ),
        cost_estimate=pl.CostEstimate(
            flops=4 * 10**9, bytes_accessed=12 * 10**6, transcendentals=10**6
        ),
    )(acts, gate, up, hid, counts, lengths, owner)


def tile_coords(tile_ids, block_count):
    block_ids = jnp.arange(block_count, dtype=jnp.int32)
    starts = block_ids * block_count - block_ids * (block_ids - 1) // 2
    row_block = jnp.sum((tile_ids[:, None] >= starts[None, :]).astype(jnp.int32), axis=1) - 1
    first_tile = jnp.sum(
        jnp.where(block_ids[None, :] == row_block[:, None], starts[None, :], 0), axis=1
    )
    return row_block, tile_ids - first_tile + row_block


def sums_before(values):
    ids = jnp.arange(values.shape[0], dtype=jnp.int32)
    return jnp.sum(jnp.where(ids[None, :] < ids[:, None], values[None, :], 0), axis=1)


def slot_weights(counts, lengths, capacity, live_total):
    slot_ids = jnp.arange(counts.shape[0] * capacity, dtype=jnp.int32)
    device_ids = jnp.arange(counts.shape[0], dtype=jnp.int32)
    match = (slot_ids // capacity)[:, None] == device_ids[None, :]
    within = slot_ids % capacity
    live_mask = within < jnp.sum(jnp.where(match, counts[None, :], 0), axis=1)
    position = within + jnp.sum(jnp.where(match, sums_before(counts)[None, :], 0), axis=1)
    begins = sums_before(lengths)
    inside = (position[:, None] >= begins[None, :]) & (
        position[:, None] < (begins + lengths)[None, :]
    )
    own = jnp.maximum(jnp.sum(jnp.where(inside, lengths[None, :], 0), axis=1), 1)
    ratio = live_total / lengths.shape[0]
    return live_mask, jnp.where(live_mask, ratio / own.astype(F32), 0.0)


def general_body(acts, gate_pre, up_pre, hidden_grad, counts, lengths, owner):
    mp_size = lax.axis_size("mp")
    dp_size = lax.axis_size("dp")
    capacity = acts.shape[0]
    live_total = mp_size * capacity - 2 * capacity
    scale = 1.0 / (dp_size * live_total)
    live_mask, weight = slot_weights(counts[0], lengths[0], capacity, live_total)
    row_block, col_block = tile_coords(owner, acts.shape[1] // TILE)
    a = gate_pre.astype(F32)
    b = up_pre.astype(F32)
    h = hidden_grad.astype(F32)
    q = jax.nn.sigmoid(a)
    w = weight[:, None]
    scaled = (
        (h * b * q * (1.0 + a * (1.0 - q)) * w).astype(BF16),
        (h * a * q * w).astype(BF16),
    )
    per = gate_pre.shape[1] // GBLK
    span = GBLK // TILE
    pieces = []
    for e in range(2):
        for block in range(per):
            for strip in range(span):
                first = block * GBLK + strip * TILE
                product = lax.dot_general(
                    scaled[e][:, first : first + TILE],
                    scaled[e][:, first : (block + 1) * GBLK],
                    (((0,), (0,)), ((), ())),
                    preferred_element_type=F32,
                )
                product = (product * scale).astype(BF16)
                pieces.append(product.reshape(TILE, span - strip, TILE).transpose(1, 0, 2))
    grad_tiles = jnp.concatenate(pieces, axis=0)
    mine = jnp.sum(
        jnp.where(
            jnp.arange(mp_size) == lax.axis_index("mp"), counts[0], 0
        )
    )
    kept = jnp.where(jnp.arange(capacity)[:, None] < mine, acts, 0)
    rows = lax.all_gather(kept, "mp", axis=0, tiled=True)

    def one_tile(pair):
        left = lax.dynamic_slice_in_dim(rows, pair[0] * TILE, TILE, 1)
        right = lax.dynamic_slice_in_dim(rows, pair[1] * TILE, TILE, 1)
        product = lax.dot_general(
            left, right, (((0,), (0,)), ((), ())), preferred_element_type=F32
        )
        return (product * scale).astype(BF16)

    act_tiles = lax.map(one_tile, (row_block, col_block))
    act_gram = lax.psum_scatter(act_tiles, "dp", scatter_dimension=1, tiled=True)
    grad_gram = lax.psum_scatter(grad_tiles, "dp", scatter_dimension=1, tiled=True)
    return act_gram, grad_gram.reshape(2, per, -1, grad_gram.shape[1], TILE)


def solution(mesh):
    fits = mesh.shape["dp"] == 2 and mesh.shape["mp"] == 16
    return jax.shard_map(
        fused_body if fits else general_body,
        mesh=mesh,
        in_specs=(
            P(("dp", "mp"), None),
            P("dp", "mp"),
            P("dp", "mp"),
            P("dp", "mp"),
            P("dp", None),
            P("dp", None),
            P("mp"),
        ),
        out_specs=(P("mp", "dp", None), P(None, "mp", None, "dp", None)),
        check_vma=False,
    )
```

time: 148 us -> 66.6 us (0.45)
  local copies, waits for them, and re-layouts: 76.8 us -> 11.2 us
  Pallas kernels: 0 us -> 54.4 us
  waiting for transfers between devices: 25.1 us -> 0 us
  matrix products: 16.7 us -> 0 us
  between operations: 15.7 us -> 0.66 us
  other arithmetic: 12 us -> 0 us
    pallas_call x0 -> x1, Pallas kernels: none -> 54.4 us  [fused_body(): pl.pallas_call(kernel, out_shape=(jax.ShapeDtypeStruct((tiles, TILE // 2,...]
    gather x2 -> x0, local copies, waits for them, and re-layouts: 18.3 us -> none  [the longest x1 9.17 us: owned_tiles(): right_rows = jnp.take(shaped, col_block, axis=0)]
    all_gather x1 -> x0, waiting for transfers between devices: 16.8 us -> none  [body(): gathered = lax.all_gather(own_columns, 'mp', axis=1, tiled=True)]
    dot_general x29 -> x0, matrix products: 16.7 us -> none  [the longest x1 8.68 us: owned_tiles(): jnp.einsum('kin,kjn->kij', left_rows, right_rows, preferred_element_type=...]
    unnamed x37 -> x18, local copies, waits for them, and re-layouts: 27.1 us -> 11.2 us
    another operation x20 -> x0, local copies, waits for them, and re-layouts: 8.37 us -> none
    reduce_scatter x2 -> x0, waiting for transfers between devices: 7.55 us -> none  [the longest x1 7.52 us: body(): lax.psum_scatter(act_tiles.astype(jnp.bfloat16), 'dp', scatter_dimension=...]
    reshape x8 -> x0, local copies, waits for them, and re-layouts: 6.74 us -> none  [gradient_tiles(): pieces.append(product.reshape(TILE, span - strip, TILE).transpose(1, 0, 2))]
  transfers between devices with their start and end apart: 3 -> 0, of which waited for: 2 -> 0; matrix products, arithmetic and copies ran while one was open for 72% -> 0% of each run, Pallas kernels for 0% -> 0%
where the time goes in v1:
time: 66.6 us; the launch traced here: 66.3 us
  Pallas kernels  54.4 us (82%)
  local copies, waits for them, and re-layouts  11.2 us (17%)
    pallas_call x1, Pallas kernels, fused_body(): pl.pallas_call(kernel, out_shape=(jax.ShapeDtypeStruct((tiles, TILE // 2,...  54.4 us
    unnamed x18, local copies, waits for them, and re-layouts  11.2 us

profile of v1, /device:TPU:0, one launch (start us, length us, event | category | flops | bytes accessed | tf_op | source)
XLA Modules:
  0.0 66.3 jit_solution(2166032544932792982)
XLA Ops:
  0.6 0.0 copy-start
  0.6 1.2 %copy-done = bf16[256,1792]{1,0:T(8,128)(2,1)S(1)} copy-done((bf16[256,1792]{1,0:T(8,128)(2,1)S(1)}, bf16[256,1792]{1,0:T(8,128)(2,1)}, u32[]{:S(2)}) %copy-start) | copy-done | bytes 917528
  1.8 0.0 copy-start.1
  1.8 1.2 %copy-done.1 = bf16[256,1792]{1,0:T(8,128)(2,1)S(1)} copy-done((bf16[256,1792]{1,0:T(8,128)(2,1)S(1)}, bf16[256,1792]{1,0:T(8,128)(2,1)}, u32[]{:S(2)}) %copy-start.1) | copy-done | bytes 917528
  3.0 0.0 copy-start.2
  3.0 1.2 %copy-done.2 = bf16[256,1792]{1,0:T(8,128)(2,1)S(1)} copy-done((bf16[256,1792]{1,0:T(8,128)(2,1)S(1)}, bf16[256,1792]{1,0:T(8,128)(2,1)}, u32[]{:S(2)}) %copy-start.2) | copy-done | bytes 917528
  4.2 0.0 copy-start.3
  4.2 0.9 %copy-done.3 = bf16[16,8192]{1,0:T(8,128)(2,1)S(1)} copy-done((bf16[16,8192]{1,0:T(8,128)(2,1)S(1)}, bf16[16,8192]{1,0:T(8,128)(2,1)}, u32[]{:S(2)}) %copy-start.3) | copy-done | bytes 262168
  5.1 0.0 copy-start.4
  5.1 0.7 %copy-done.4 = s32[130]{0:T(256)S(1)} copy-done((s32[130]{0:T(256)S(1)}, s32[130]{0:T(256)}, u32[]{:S(2)}) %copy-start.4) | copy-done | bytes 544
  5.8 0.0 copy-start.5
  5.8 0.7 copy-done.5
  6.5 0.0 copy-start.6
  6.5 0.7 copy-done.6
  7.1 54.4 %shard_map.86 = (bf16[130,64,128]{2,1,0:T(8,128)(2,1)}, bf16[2,2,28,64,128]{4,3,2,1,0:T(8,128)(2,1)}) custom-call(bf16[16,8192]{1,0:T(8,128)(2,1)S(1)} %copy-done.3, bf16[256,1792]{1,0:T(8,128)(2,1)S(1)} %copy-done, bf16[256,1792]{1,0:T(8,128)(2,1)S(1)} %copy-done.1, bf16[256,1792]{1,0:T(8,128)(2,1)S(1)} %copy-done.2, s32[1,16]{1,0:T(1,128)S(1)} %copy-done.5, ...), custom_call_target="tpu_custom_call" | custom-call | flops 4000000000 | bytes 12000000 | tf_op jit(solution)/shard_map/pallas_call | solution.py:395
  61.5 0.0 copy-start.7
  61.5 3.5 %copy.11 = bf16[130,64,128]{2,1,0:T(8,128)(2,1)} copy(bf16[130,64,128]{2,1,0:T(8,128)(2,1)} %get-tuple-element.4) | data formatting | bytes 4259840
  65.0 0.0 copy-done.7
  65.0 1.2 %copy.12 = bf16[2,2,28,64,128]{4,3,2,1,0:T(8,128)(2,1)} copy(bf16[2,2,28,64,128]{4,3,2,1,0:T(8,128)(2,1)S(1)} %copy-done.7) | data formatting | bytes 3670016
Async XLA Ops:
  0.6 1.2 %copy-start = (bf16[256,1792]{1,0:T(8,128)(2,1)S(1)}, bf16[256,1792]{1,0:T(8,128)(2,1)}, u32[]{:S(2)}) copy-start(bf16[256,1792]{1,0:T(8,128)(2,1)} %gate_in.1) | copy-start | bytes 2752516
  1.8 1.2 %copy-start.1 = (bf16[256,1792]{1,0:T(8,128)(2,1)S(1)}, bf16[256,1792]{1,0:T(8,128)(2,1)}, u32[]{:S(2)}) copy-start(bf16[256,1792]{1,0:T(8,128)(2,1)} %up_in.1) | copy-start | bytes 2752516
  3.0 1.2 %copy-start.2 = (bf16[256,1792]{1,0:T(8,128)(2,1)S(1)}, bf16[256,1792]{1,0:T(8,128)(2,1)}, u32[]{:S(2)}) copy-start(bf16[256,1792]{1,0:T(8,128)(2,1)} %hid_in.1) | copy-start | bytes 2752516
  4.2 0.9 %copy-start.3 = (bf16[16,8192]{1,0:T(8,128)(2,1)S(1)}, bf16[16,8192]{1,0:T(8,128)(2,1)}, u32[]{:S(2)}) copy-start(bf16[16,8192]{1,0:T(8,128)(2,1)} %act_in.1) | copy-start | bytes 786436
  5.1 0.7 %copy-start.4 = (s32[130]{0:T(256)S(1)}, s32[130]{0:T(256)}, u32[]{:S(2)}) copy-start(s32[130]{0:T(256)} %owner.1) | copy-start | bytes 1564
  5.8 0.7 copy-start.5
  6.5 0.7 copy-start.6
  61.5 3.5 %copy-start.7 = (bf16[2,2,28,64,128]{4,3,2,1,0:T(8,128)(2,1)S(1)}, bf16[2,2,28,64,128]{4,3,2,1,0:T(8,128)(2,1)}, u32[]{:S(2)}) copy-start(bf16[2,2,28,64,128]{4,3,2,1,0:T(8,128)(2,1)} %get-tuple-element.5) | copy-start | bytes 5505028

commit v2 on v1

--- a/solution.py
+++ b/solution.py
@@ -25,11 +25,14 @@
     gate_in,
     up_in,
     hid_in,
+    counts_in,
+    lengths_in,
+    owner_in,
+    act_out,
+    grad_out,
     counts,
     lengths,
     owner,
-    act_out,
-    grad_out,
     own_raw,
     gate,
     up,
@@ -83,15 +86,19 @@
     xy_of_d = (1 - y) * 2 + (1 - x)
 
     loads = [
+        pltpu.make_async_copy(counts_in, counts, in_sem.at[4]),
         pltpu.make_async_copy(act_in, own_raw, in_sem.at[0]),
         pltpu.make_async_copy(gate_in, gate, in_sem.at[1]),
         pltpu.make_async_copy(up_in, up, in_sem.at[2]),
         pltpu.make_async_copy(hid_in, hid, in_sem.at[3]),
+        pltpu.make_async_copy(lengths_in, lengths, in_sem.at[5]),
+        pltpu.make_async_copy(owner_in, owner, in_sem.at[6]),
     ]
     for copy in loads:
         copy.start()
 
     loads[0].wait()
+    loads[1].wait()
     live = counts[0, me]
     row_live = lax.broadcasted_iota(jnp.int32, (cap, TILE), 0) < live
 
@@ -155,6 +162,9 @@
     @pl.when(is_mid)
     def _():
         z_copy(z, z3, 1, 1).start()
+
+    for copy in loads[2:]:
+        copy.wait()
 
     within = lax.broadcasted_iota(jnp.int32, (cap, TILE), 0)
     seqs = lengths.shape[1]
@@ -177,8 +187,6 @@
 
     lax.fori_loop(0, counts.shape[1], put_weight, jnp.int32(0))
 
-    for copy in loads[1:]:
-        copy.wait()
     per = sc.shape[1]
     span = GBLK // TILE
     rows = gate.shape[0]
@@ -387,7 +395,7 @@
     chunk = largest_divisor(tiles, 10)
     chunks = tiles // chunk
     anywhere = pl.BlockSpec(memory_space=pl.ANY)
-    smem = pl.BlockSpec(memory_space=pltpu.SMEM)
+    in_hbm = pl.BlockSpec(memory_space=pltpu.HBM)
     dma = pltpu.SemaphoreType.DMA
     kernel = functools.partial(
         fused_kernel, 1.0 / (2 * live_total), live_total / lengths.shape[1]
@@ -398,9 +406,12 @@
             jax.ShapeDtypeStruct((tiles, TILE // 2, TILE), BF16),
             jax.ShapeDtypeStruct((2, per, pairs, TILE // 2, TILE), BF16),
         ),
-        in_specs=[anywhere] * 4 + [smem] * 3,
+        in_specs=[in_hbm] * 7,
         out_specs=(anywhere, anywhere),
         scratch_shapes=[
+            pltpu.SMEM(counts.shape, jnp.int32),
+            pltpu.SMEM(lengths.shape, jnp.int32),
+            pltpu.SMEM(owner.shape, jnp.int32),
             pltpu.VMEM((cap, width), BF16),
             pltpu.VMEM(gate.shape, BF16),
             pltpu.VMEM(gate.shape, BF16),
@@ -418,7 +429,7 @@
             pltpu.VMEM((2 * per, pairs, TILE // 2, TILE), BF16),
             pltpu.VMEM((chunks, chunk, TILE // 2, TILE), BF16),
             pltpu.VMEM((2 * per, pairs, TILE // 2, TILE), BF16),
-            dma((4,)),
+            dma((7,)),
             dma((chunks,)),
             dma((2 * per,)),
             dma((5,)),
@@ -433,12 +444,17 @@
             dma((chunks,)),
         ],
         compiler_params=pltpu.CompilerParams(
-            collective_id=0, has_side_effects=True, vmem_limit_bytes=50 * 2**20
+            collective_id=0, has_side_effects=True, vmem_limit_bytes=36 * 2**20
         ),
         cost_estimate=pl.CostEstimate(
             flops=4 * 10**9, bytes_accessed=12 * 10**6, transcendentals=10**6
         ),
-    )(acts, gate, up, hid, counts, lengths, owner)
+    )(
+        *(
+            pltpu.with_memory_space_constraint(array, pltpu.HBM)
+            for array in (acts, gate, up, hid, counts, lengths, owner)
+        )
+    )
 
 
 def tile_coords(tile_ids, block_count):

time: 66.6 us -> 58.2 us (0.87)
  local copies, waits for them, and re-layouts: 11.2 us -> 2.56 us
    unnamed x18 -> x2, local copies, waits for them, and re-layouts: 11.2 us -> 2.56 us
where the time goes in v2:
time: 58.2 us; the launch traced here: 58.1 us
  Pallas kernels  54.9 us (94%)
  local copies, waits for them, and re-layouts  2.56 us (4%)
  between operations  0.64 us (1%)
    pallas_call x1, Pallas kernels, fused_body(): pl.pallas_call(kernel, out_shape=(jax.ShapeDtypeStruct((tiles, TILE // 2,...  54.9 us
    unnamed x2, local copies, waits for them, and re-layouts  2.56 us

profile of v2, /device:TPU:0, one launch (start us, length us, event | category | flops | bytes accessed | tf_op | source)
XLA Modules:
  0.0 58.1 jit_solution(12066680266409947285)
XLA Ops:
  0.6 54.9 %shard_map.86 = (bf16[130,64,128]{2,1,0:T(8,128)(2,1)S(1)}, bf16[2,2,28,64,128]{4,3,2,1,0:T(8,128)(2,1)S(1)}) custom-call(bf16[16,8192]{1,0:T(8,128)(2,1)} %act_in.1, bf16[256,1792]{1,0:T(8,128)(2,1)} %gate_in.1, bf16[256,1792]{1,0:T(8,128)(2,1)} %up_in.1, bf16[256,1792]{1,0:T(8,128)(2,1)} %hid_in.1, s32[1,16]{1,0:T(1,128)} %counts_in.1, s32[1,4]{1,0:T(1,128)} %lengths_in.1, ...), custom_call_target="tpu_custom_call" | custom-call | flops 4000000000 | bytes 12000000 | tf_op jit(solution)/shard_map/pallas_call | solution.py:403
  55.5 1.3 %copy.11 = bf16[130,64,128]{2,1,0:T(8,128)(2,1)} copy(bf16[130,64,128]{2,1,0:T(8,128)(2,1)S(1)} %get-tuple-element.4) | data formatting | bytes 4259840
  56.9 1.2 %copy.12 = bf16[2,2,28,64,128]{4,3,2,1,0:T(8,128)(2,1)} copy(bf16[2,2,28,64,128]{4,3,2,1,0:T(8,128)(2,1)S(1)} %get-tuple-element.5) | data formatting | bytes 3670016

commit v3 on v2

--- a/solution.py
+++ b/solution.py
@@ -37,7 +37,8 @@
     gate,
     up,
     hid,
-    xs,
+    near,
+    far,
     xt,
     sc,
     sct,
@@ -77,9 +78,16 @@
     z3 = 3 - z
     mid = ((z + 1) // 2) % 2
     is_mid = mid == 1
-    zorder = (z, z1, mid * z3 + (1 - mid) * z2, mid * z2 + (1 - mid) * z3)
     cap = act_in.shape[0]
-    blocks = xs.shape[1]
+    blocks = near.shape[1]
+
+    def place(item, slot_xy):
+        return (near, far)[item // 2], (item % 2) * 4 + slot_xy
+
+    def slot_of(item, slot_xy):
+        ref, index = place(item, slot_xy)
+        return ref.at[index]
+
     half = blocks // 2
     xy_of_xn = y * 2 + (1 - x)
     xy_of_yn = (1 - y) * 2 + x
@@ -104,7 +112,7 @@
 
     def put_own(b, carry):
         value = own_raw[:, pl.ds(pl.multiple_of(b * TILE, TILE), TILE)]
-        xs[me, b] = jnp.where(row_live, value.astype(F32), 0.0).astype(BF16)
+        near[xy, b] = jnp.where(row_live, value.astype(F32), 0.0).astype(BF16)
         return carry
 
     lax.fori_loop(0, blocks, put_own, 0, unroll=8)
@@ -121,22 +129,23 @@
 
     pl.semaphore_wait(barrier, 4 + mid)
 
-    def z_copy(src_z, target_z, index, which):
-        slot = xs.at[src_z * 4 + xy]
+    def z_copy(src_item, target_z, index, which):
         return pltpu.make_async_remote_copy(
-            src_ref=slot, dst_ref=slot, send_sem=zs.at[index], recv_sem=zr.at[which],
+            src_ref=slot_of(src_item, xy), dst_ref=slot_of(which + 1, xy),
+            send_sem=zs.at[index], recv_sem=zr.at[which],
             device_id=(g, target_z * 4 + xy), device_id_type=MESH,
         )
 
     def full_copy(way, item, slot_xy, target):
-        slot = xs.at[zorder[item] * 4 + slot_xy]
+        slot = slot_of(item, slot_xy)
         return pltpu.make_async_remote_copy(
             src_ref=slot, dst_ref=slot, send_sem=fs.at[way, item], recv_sem=fr.at[way, item],
             device_id=(g, target), device_id_type=MESH,
         )
 
     def half_copy(way, item, slot_xy, target):
-        slot = xs.at[zorder[item] * 4 + slot_xy, pl.ds(way * half, half)]
+        ref, index = place(item, slot_xy)
+        slot = ref.at[index, pl.ds(way * half, half)]
         return pltpu.make_async_remote_copy(
             src_ref=slot, dst_ref=slot, send_sem=hs.at[way, item], recv_sem=hr.at[way, item],
             device_id=(g, target), device_id_type=MESH,
@@ -156,12 +165,12 @@
         half_copy(0, item, xy_of_d, xn).wait_recv()
         half_copy(1, item, xy_of_d, yn).wait_recv()
 
-    z_copy(z, z1, 0, 0).start()
+    z_copy(0, z1, 0, 0).start()
     send_item(0)
 
     @pl.when(is_mid)
     def _():
-        z_copy(z, z3, 1, 1).start()
+        z_copy(0, z3, 1, 1).start()
 
     for copy in loads[2:]:
         copy.wait()
@@ -213,12 +222,12 @@
 
     lax.fori_loop(0, per * span, scaled_block, 0)
 
-    z_copy(z1, z1, 0, 0).wait_recv()
+    z_copy(0, z1, 0, 0).wait_recv()
     send_item(1)
 
     @pl.when(is_mid)
     def _():
-        z_copy(z1, z3, 2, 2).start()
+        z_copy(1, z3, 2, 2).start()
 
     pass_halves(0)
 
@@ -244,21 +253,21 @@
 
     lax.fori_loop(0, 2 * per, grad_tiles, 0)
 
-    z_copy(zorder[2], z1, 0, 1).wait_recv()
+    z_copy(2, z1, 0, 1).wait_recv()
     send_item(2)
 
     @pl.when(is_mid)
     def _():
-        z_copy(z3, z1, 1 + 2, 1).start()
+        z_copy(2, z1, 3, 1).start()
 
     pass_halves(1)
 
-    z_copy(zorder[3], z1, 0, 2).wait_recv()
+    z_copy(3, z1, 0, 2).wait_recv()
     send_item(3)
 
     @pl.when(is_mid)
     def _():
-        z_copy(z2, z1, 4, 2).start()
+        z_copy(3, z1, 4, 2).start()
 
     tiles = owner.shape[0]
 
@@ -299,18 +308,18 @@
 
     def transpose_half(which):
         def one(b, carry):
-            block = xs[pl.ds(which * group, group), b].reshape(group * cap, TILE)
-            xt[b, :, pl.ds(pl.multiple_of(which * TILE, TILE), TILE)] = block.T
+            block = (near, far)[which][:, b].reshape(group * cap, TILE)
+            xt[b, :, which * TILE : (which + 1) * TILE] = block.T
             return carry
 
         lax.fori_loop(0, blocks, one, 0, unroll=4)
 
     pass_halves(2)
     lax.fori_loop(0, 2 * per, grad_finish, 0)
+    transpose_half(0)
     pass_halves(3)
     take_halves(2)
     take_halves(3)
-    transpose_half(0)
     transpose_half(1)
 
     chunks = part_a.shape[0]
@@ -332,7 +341,10 @@
         for i in range(width):
             k = n * width + i
             left = xt[rb[k]]
-            right = xs[:, cb[k]].reshape(2 * TILE, TILE)
+            c = cb[k]
+            right = jnp.concatenate(
+                [ref[:, c].reshape(TILE, TILE) for ref in (near, far)], axis=0
+            )
             tile = jnp.dot(left, right, preferred_element_type=F32)
             part_a[n, i] = (tile * scale).astype(BF16)
         act_send(n).start()
@@ -355,14 +367,14 @@
     lax.fori_loop(2, chunks, act_both, 0)
     lax.fori_loop(chunks - 2, chunks, act_finish, 0)
 
-    z_copy(z, z1, 0, 0).wait_send()
+    z_copy(0, z1, 0, 0).wait_send()
 
     @pl.when(is_mid)
     def _():
-        z_copy(z, z3, 1, 1).wait_send()
-        z_copy(z1, z3, 2, 2).wait_send()
-        z_copy(z3, z1, 3, 1).wait_send()
-        z_copy(z2, z1, 4, 2).wait_send()
+        z_copy(0, z3, 1, 1).wait_send()
+        z_copy(1, z3, 2, 2).wait_send()
+        z_copy(2, z1, 3, 1).wait_send()
+        z_copy(3, z1, 4, 2).wait_send()
 
     for item in range(4):
         full_copy(0, item, xy, xn).wait_send()
@@ -416,7 +428,8 @@
             pltpu.VMEM(gate.shape, BF16),
             pltpu.VMEM(gate.shape, BF16),
             pltpu.VMEM(gate.shape, BF16),
-            pltpu.VMEM((slots, blocks, cap, TILE), BF16),
+            pltpu.VMEM((slots // 2, blocks, cap, TILE), BF16),
+            pltpu.VMEM((slots // 2, blocks, cap, TILE), BF16),
             pltpu.VMEM((blocks, TILE, rows), BF16),
             pltpu.VMEM((2, per, span, rows, TILE), BF16),
             pltpu.VMEM((2, per, span, TILE, rows), BF16),

time: 58.2 us -> 56.8 us (0.976)
  Pallas kernels: 54.9 us -> 53.5 us
    pallas_call x1, Pallas kernels: 54.9 us -> 53.5 us  [fused_body(): pl.pallas_call(kernel, out_shape=(jax.ShapeDtypeStruct((tiles, TILE // 2,...]
where the time goes in v3:
time: 56.8 us; the launch traced here: 56.7 us
  Pallas kernels  53.5 us (94%)
  local copies, waits for them, and re-layouts  2.56 us (5%)
  between operations  0.64 us (1%)
    pallas_call x1, Pallas kernels, fused_body(): pl.pallas_call(kernel, out_shape=(jax.ShapeDtypeStruct((tiles, TILE // 2,...  53.5 us
    unnamed x2, local copies, waits for them, and re-layouts  2.56 us

profile of v3, /device:TPU:0, one launch (start us, length us, event | category | flops | bytes accessed | tf_op | source)
XLA Modules:
  0.0 56.7 jit_solution(3191427376659812804)
XLA Ops:
  0.6 53.5 %shard_map.86 = (bf16[130,64,128]{2,1,0:T(8,128)(2,1)S(1)}, bf16[2,2,28,64,128]{4,3,2,1,0:T(8,128)(2,1)S(1)}) custom-call(bf16[16,8192]{1,0:T(8,128)(2,1)} %act_in.1, bf16[256,1792]{1,0:T(8,128)(2,1)} %gate_in.1, bf16[256,1792]{1,0:T(8,128)(2,1)} %up_in.1, bf16[256,1792]{1,0:T(8,128)(2,1)} %hid_in.1, s32[1,16]{1,0:T(1,128)} %counts_in.1, s32[1,4]{1,0:T(1,128)} %lengths_in.1, ...), custom_call_target="tpu_custom_call" | custom-call | flops 4000000000 | bytes 12000000 | tf_op jit(solution)/shard_map/pallas_call | solution.py:415
  54.1 1.3 %copy.11 = bf16[130,64,128]{2,1,0:T(8,128)(2,1)} copy(bf16[130,64,128]{2,1,0:T(8,128)(2,1)S(1)} %get-tuple-element.4) | data formatting | bytes 4259840
  55.4 1.2 %copy.12 = bf16[2,2,28,64,128]{4,3,2,1,0:T(8,128)(2,1)} copy(bf16[2,2,28,64,128]{4,3,2,1,0:T(8,128)(2,1)S(1)} %get-tuple-element.5) | data formatting | bytes 3670016
